TPU v7x, 1024 devices: a whole 8x8x8 slice. The times are simulated.
1024 devices in a mesh: row: 32 (over x, z_hi, core), col: 32 (over z_lo, y).
Axes of the slice: x: 8, y: 8, z: 8 (z_hi: 2, z_lo: 4; z = z_hi * 4 + z_lo), core: 2. Of those that a mesh axis runs over, the one named last changes fastest.
Arguments:
- a_blocks: float32 [32, 32, 3, 256, 256], P('row', 'col'), may hold values from -1.5 to 1.5
- a_positions: int32 [32, 32, 3], P('row', 'col'), may hold values from 0 to 4, as said below
- b_blocks: float32 [32, 32, 3, 256, 256], P('row', 'col'), may hold values from -1.5 to 1.5
- b_positions: int32 [32, 32, 3], P('row', 'col'), may hold values from 0 to 4, as said below
Outputs:
- product: float32 [16384, 16384], P('row', 'col')
Inputs may be any that keep to these rules, and one draw needn't show every extreme that they name: `a_positions`: in each device's list the filled slots come first and name distinct tile positions; the value 2 * 2 marks an empty slot; every device has one filled slot or more, some device has all 3 filled and some device exactly one. `b_positions`: as for a_positions.
All inputs are finite; a program needn't handle non-finite values.
Results may differ from a plain program's by a relative error of at most 0.0003.
Values sent between devices are 32-bit elements; how exact they have to be, the bound alone decides.
A program may use at most 32 MiB of HBM per device.

v0:
```python
import jax
import jax.numpy as jnp
from jax import lax
from jax.sharding import PartitionSpec as P

BLK = 256
TB = 2


def passed_along(shard, axis, by):
    peers = lax.axis_size(axis)
    return lax.ppermute(shard, axis, [(i, (i + by) % peers) for i in range(peers)])


def densify(blocks, positions):
    cells = TB * TB
    onehot = (positions[..., None] == jnp.arange(cells, dtype=jnp.int32)).astype(jnp.float32)
    tiles = jnp.einsum("sp,sxy->pxy", onehot, blocks, precision=lax.Precision.HIGHEST)
    tiles = tiles.reshape(TB, TB, BLK, BLK).transpose(0, 2, 1, 3)
    return tiles.reshape(TB * BLK, TB * BLK)


def matmul(left, right):
    return jnp.dot(left, right, precision=lax.Precision.HIGHEST, preferred_element_type=jnp.float32)


def body(a_blocks, a_positions, b_blocks, b_positions):
    a_list = a_blocks[0, 0]
    b_list = b_blocks[0, 0]
    a_where = a_positions[0, 0]
    b_where = b_positions[0, 0]
    a_own = densify(a_list, a_where)
    b_own = densify(b_list, b_where)
    a_next = passed_along(a_own, "col", -1)
    b_next = passed_along(b_own, "row", -1)
    return matmul(a_own, b_own) + matmul(a_next, b_next)


def solution(mesh):
    placed = (
        P("row", "col", None, None, None),
        P("row", "col", None),
        P("row", "col", None, None, None),
        P("row", "col", None),
    )
    return jax.shard_map(
        body, mesh=mesh, in_specs=placed, out_specs=P("row", "col"), check_vma=False
    )
```

profile of v0, /device:TPU:119, one launch (start us, length us, event | category | flops | bytes accessed | tf_op | source)
XLA Modules:
  0.0 74.3 jit_solution(4909338087093144340)
XLA Ops:
  0.0 0.0 copy-start.1
  0.0 0.7 copy-done.1
  0.7 3.1 %fusion.2 = f32[2,2,256,256]{3,1,2,0:T(2,128)S(1)} fusion(f32[3,256,256]{2,1,0:T(8,128)} %bitcast.38, s32[2,2]{1,0:T(2,128)S(1)} %multiply_add_fusion, s32[3]{0:T(128)S(1)} %bitcast.40), kind=kOutput, calls=%fused_computation.3 | convolution fusion | flops 9437196 | bytes 1835036 | tf_op jit(solution)/shard_map/sp,sxy->pxy/dot_general | solution.py:18
  3.8 0.0 copy-start
  3.8 0.1 copy.9
  3.9 3.0 %collective-permute-start = (f32[512,512]{1,0:T(8,128)S(1)}, f32[512,512]{1,0:T(8,128)S(1)}, u32[]{:S(2)}, u32[]{:S(2)}) collective-permute-start(f32[512,512]{1,0:T(8,128)S(1)} %bitcast.32), channel_id=1, source_target_pairs={{0,31},{1,0},{2,1},{3,2},{4,3},{5,4},{6,5},{7,6},{8,7},{9,8},{10,9... | collective-permute-start | bytes 3145736 | tf_op jit(solution)/shard_map/ppermute | solution.py:12
  6.9 0.0 copy-start.2
  6.9 0.0 copy-done
  6.9 0.6 copy-done.2
  7.6 2.0 %fusion = f32[2,2,256,256]{3,1,2,0:T(2,128)S(1)} fusion(f32[3,256,256]{2,1,0:T(8,128)S(1)} %bitcast.39, s32[3]{0:T(128)S(1)} %bitcast.41, s32[2,2]{1,0:T(2,128)S(1)} %multiply_add_fusion), kind=kOutput, calls=%fused_computation.1 | convolution fusion | flops 9437196 | bytes 1835036 | tf_op jit(solution)/shard_map/sp,sxy->pxy/dot_general | solution.py:18
  9.6 0.1 copy.10
  9.7 2.9 %collective-permute-start.1 = (f32[512,512]{1,0:T(8,128)S(1)}, f32[512,512]{1,0:T(8,128)S(1)}, u32[]{:S(2)}, u32[]{:S(2)}) collective-permute-start(f32[512,512]{1,0:T(8,128)S(1)} %bitcast.34), channel_id=1, source_target_pairs={{0,992},{32,0},{64,32},{96,64},{128,96},{160,128},{192,160},{224,1... | collective-permute-start | bytes 3145736 | tf_op jit(solution)/shard_map/ppermute | solution.py:12
  12.5 1.9 %fusion.14 = f32[512,512]{1,0:T(8,128)S(1)} fusion(f32[512,512]{1,0:T(8,128)S(1)} %bitcast.33, f32[512,512]{1,0:T(8,128)S(1)} %bitcast.35), kind=kOutput, calls=%fused_computation.16 | convolution fusion | flops 1610612736 | bytes 3145728 | tf_op jit(solution)/shard_map/dot_general | solution.py:24
  14.4 19.5 %collective-permute-done = f32[512,512]{1,0:T(8,128)S(1)} collective-permute-done((f32[512,512]{1,0:T(8,128)S(1)}, f32[512,512]{1,0:T(8,128)S(1)}, u32[]{:S(2)}, u32[]{:S(2)}) %collective-permute-start) | collective-permute-done | bytes 1048608 | tf_op jit(solution)/shard_map/ppermute | solution.py:12
  33.9 37.6 %collective-permute-done.1 = f32[512,512]{1,0:T(8,128)S(1)} collective-permute-done((f32[512,512]{1,0:T(8,128)S(1)}, f32[512,512]{1,0:T(8,128)S(1)}, u32[]{:S(2)}, u32[]{:S(2)}) %collective-permute-start.1) | collective-permute-done | bytes 1048608 | tf_op jit(solution)/shard_map/ppermute | solution.py:12
  71.5 2.8 %convolution_add_fusion = f32[512,512]{1,0:T(8,128)} fusion(f32[512,512]{1,0:T(8,128)S(1)} %fusion.14, f32[512,512]{1,0:T(8,128)S(1)} %collective-permute-done, f32[512,512]{1,0:T(8,128)S(1)} %collective-permute-done.1), kind=kOutput, calls=%fused_computation | convolution fusion | flops 1610874880 | bytes 4194304 | tf_op jit(solution)/shard_map/dot_general | solution.py:24
  (1 shorter events, 0.0 us)
Async XLA Ops:
  0.0 0.7 copy-start.1
  3.8 3.1 %copy-start = (f32[1,1,3,256,256]{4,3,2,1,0:T(8,128)S(1)}, f32[1,1,3,256,256]{4,3,2,1,0:T(8,128)}, u32[]{:S(2)}) copy-start(f32[1,1,3,256,256]{4,3,2,1,0:T(8,128)} %param.6) | copy-start | bytes 2359300
  3.9 30.0 %collective-permute-start = (f32[512,512]{1,0:T(8,128)S(1)}, f32[512,512]{1,0:T(8,128)S(1)}, u32[]{:S(2)}, u32[]{:S(2)}) collective-permute-start(f32[512,512]{1,0:T(8,128)S(1)} %bitcast.32), channel_id=1, source_target_pairs={{0,31},{1,0},{2,1},{3,2},{4,3},{5,4},{6,5},{7,6},{8,7},{9,8},{10,9... | collective-permute-start | bytes 3145736 | tf_op jit(solution)/shard_map/ppermute | solution.py:12
  6.9 0.7 copy-start.2
  9.7 61.8 %collective-permute-start.1 = (f32[512,512]{1,0:T(8,128)S(1)}, f32[512,512]{1,0:T(8,128)S(1)}, u32[]{:S(2)}, u32[]{:S(2)}) collective-permute-start(f32[512,512]{1,0:T(8,128)S(1)} %bitcast.34), channel_id=1, source_target_pairs={{0,992},{32,0},{64,32},{96,64},{128,96},{160,128},{192,160},{224,1... | collective-permute-start | bytes 3145736 | tf_op jit(solution)/shard_map/ppermute | solution.py:12
where the time goes:
time: 74.6 us; the launch traced here: 74.3 us
  waiting for transfers between devices  57.1 us (77%)
  matrix products  9.83 us (13%)
  starting transfers between devices  5.86 us (8%)
  local copies, waits for them, and re-layouts  1.44 us (2%)
    ppermute x2, waiting for transfers between devices, passed_along(): lax.ppermute(shard, axis, [(i, (i + by) % peers) for i in range(peers)])  57.1 us
    ppermute x2, starting transfers between devices, passed_along(): lax.ppermute(shard, axis, [(i, (i + by) % peers) for i in range(peers)])  5.86 us
    dot_general x2, matrix products, densify(): jnp.einsum('sp,sxy->pxy', onehot, blocks, precision=lax.Precision.HIGHEST)  5.16 us
    dot_general x2, matrix products, matmul(): jnp.dot(left, right, precision=lax.Precision.HIGHEST, preferred_element_t...  4.67 us
  transfers between devices with their start and end apart: 2, of which 2 were waited for; matrix products, arithmetic and copies ran while one was open for 5% of the time, Pallas kernels for 0%

commit v1 on v0

v1 whole, which is shorter than its diff:
```python
import jax
import jax.numpy as jnp
from jax import lax
from jax.experimental import pallas as pl
from jax.experimental.pallas import tpu as pltpu
from jax.sharding import PartitionSpec as P

BLK = 256
TB = 2
SLOTS = 3
SIDE = BLK * TB
MESH = pl.DeviceIdType.MESH


def place():
    r, c = lax.axis_index("row"), lax.axis_index("col")
    return r // 4, c % 8, (r // 2) % 2 * 4 + c // 8, r % 2


def device(x, y, z, core):
    x, y, z = (v % 8 for v in (x, y, z))
    return (x * 4 + z // 4 * 2 + core, z % 4 * 8 + y)


def along(rows, cols):
    r, c = lax.axis_index("row"), lax.axis_index("col")
    return ((r + rows) % 32, (c + cols) % 32)


def signal(sem, target):
    pl.semaphore_signal(sem, inc=1, device_id=target, device_id_type=MESH)


def densify(slots, where, high, low):
    positions = where[...]
    for p in range(TB * TB):
        r, k = p // TB, p % TB
        chosen = [(positions[:, s : s + 1] == p).astype(jnp.float32) for s in range(SLOTS)]
        block = chosen[0] * slots[0] + chosen[1] * slots[1] + chosen[2] * slots[2]
        top = block.astype(jnp.bfloat16)
        rest = (block - top.astype(jnp.float32)).astype(jnp.bfloat16)
        spot = (pl.ds(r * BLK, BLK), pl.ds(k * BLK, BLK))
        high[spot] = top
        low[spot] = rest


def product(left, right, c):
    cols = pl.ds(c * BLK, BLK)
    (lh, ll), (rh, rl) = left, right

    def dot(u, v):
        return jnp.dot(u, v, preferred_element_type=jnp.float32)

    return dot(lh[...], rh[:, cols]) + dot(lh[...], rl[:, cols]) + dot(ll[...], rh[:, cols])


def kernel(a, a_pos, b, b_pos, out, a_own, b_own, a_in, b_in, where, tiles, load, send, recv, ready):
    x, y, z, core = place()
    far = core == 0
    upper = z >= 4
    barrier = pltpu.get_barrier_semaphore()

    local = [
        pltpu.make_async_copy(a, a_own, load.at[0]),
        pltpu.make_async_copy(b, b_own, load.at[1]),
        pltpu.make_async_copy(a_pos, where.at[0], load.at[2]),
        pltpu.make_async_copy(b_pos, where.at[1], load.at[3]),
    ]
    for copy in local:
        copy.start()

    a_to, a_from = along(0, -1), along(0, 1)
    b_to, b_from = along(-1, 0), along(1, 0)

    def outgoing(src, dst, which, slot, target):
        return pltpu.make_async_remote_copy(
            src_ref=src,
            dst_ref=dst,
            send_sem=send.at[which, slot],
            recv_sem=recv.at[which, slot],
            device_id=target,
            device_id_type=MESH,
        )

    a_sends = [outgoing(a_pos, where.at[2], 0, SLOTS, a_to)]
    a_sends += [outgoing(a.at[s], a_in.at[s], 0, s, a_to) for s in range(SLOTS)]
    b_sends = [outgoing(b_pos, where.at[3], 1, SLOTS, b_to)]
    b_sends += [outgoing(b.at[s], b_in.at[s], 1, s, b_to) for s in range(SLOTS)]

    def start(copies):
        for copy in copies:
            copy.start()

    signal(barrier, a_from)

    @pl.when(far)
    def _():
        @pl.when(jnp.logical_not(upper))
        def _():
            signal(barrier, b_to)
            pl.semaphore_wait(barrier, 2)

        @pl.when(upper)
        def _():
            pl.semaphore_wait(barrier, 3)

        signal(ready, b_from)
        start(a_sends)

        @pl.when(upper)
        def _():
            start(b_sends)

    @pl.when(jnp.logical_not(far))
    def _():
        signal(barrier, b_to)

        @pl.when(jnp.logical_not(upper))
        def _():
            signal(barrier, b_from)
            pl.semaphore_wait(barrier, 1)

        @pl.when(upper)
        def _():
            pl.semaphore_wait(barrier, 2)
            signal(ready, b_from)

        start(a_sends)
        pl.semaphore_wait(ready, 1)
        start(b_sends)

    for copy in local:
        copy.wait()
    ah, al, bh, bl = (tiles.at[i] for i in range(4))
    densify(a_own, where.at[0], ah, al)
    densify(b_own, where.at[1], bh, bl)
    for c in range(TB):
        out[:, pl.ds(c * BLK, BLK)] = product((ah, al), (bh, bl), c)

    @pl.when(jnp.logical_and(far, jnp.logical_not(upper)))
    def _():
        pl.semaphore_wait(ready, 1)
        start(b_sends)

    for copy in a_sends:
        copy.wait_recv()
    densify(a_in, where.at[2], ah, al)
    for copy in b_sends:
        copy.wait_recv()
    densify(b_in, where.at[3], bh, bl)
    for c in range(TB):
        out[:, pl.ds(c * BLK, BLK)] += product((ah, al), (bh, bl), c)
    for copy in a_sends + b_sends:
        copy.wait_send()


def body(a_blocks, a_positions, b_blocks, b_positions):
    held = pltpu.VMEM((SLOTS, BLK, BLK), jnp.float32)
    return pl.pallas_call(
        kernel,
        out_shape=jax.ShapeDtypeStruct((SIDE, SIDE), jnp.float32),
        in_specs=[pl.BlockSpec(memory_space=pltpu.HBM)] * 4,
        out_specs=pl.BlockSpec(memory_space=pltpu.VMEM),
        scratch_shapes=[
            held,
            held,
            held,
            held,
            pltpu.VMEM((4, 1, SLOTS), jnp.int32),
            pltpu.VMEM((4, SIDE, SIDE), jnp.bfloat16),
            pltpu.SemaphoreType.DMA((4,)),
            pltpu.SemaphoreType.DMA((2, SLOTS + 1)),
            pltpu.SemaphoreType.DMA((2, SLOTS + 1)),
            pltpu.SemaphoreType.REGULAR,
        ],
        compiler_params=pltpu.CompilerParams(
            collective_id=0, has_side_effects=True, vmem_limit_bytes=40 * 1024 * 1024
        ),
    )(a_blocks[0, 0], a_positions[0], b_blocks[0, 0], b_positions[0])


def solution(mesh):
    placed = (
        P("row", "col", None, None, None),
        P("row", "col", None),
        P("row", "col", None, None, None),
        P("row", "col", None),
    )
    return jax.shard_map(body, mesh=mesh, in_specs=placed, out_specs=P("row", "col"), check_vma=False)
```

time: 74.6 us -> 55.6 us (0.75)
  the two profiles are of different devices: /device:TPU:119 before, /device:TPU:115 now
where the time goes in v1:
time: 55.6 us; the launch traced here: 55.4 us
  Pallas kernels  51.4 us (92%)
  local copies, waits for them, and re-layouts  3.91 us (7%)
    pallas_call x1, Pallas kernels, body(): pl.pallas_call(kernel, out_shape=jax.ShapeDtypeStruct((SIDE, SIDE), jnp.f...  51.4 us
    unnamed x9, local copies, waits for them, and re-layouts  3.91 us

profile of v1, /device:TPU:115, one launch (start us, length us, event | category | flops | bytes accessed | tf_op | source)
XLA Modules:
  0.0 55.4 jit_solution(17488248197167105584)
XLA Ops:
  0.0 0.0 copy-start.2
  0.0 0.0 copy-start.3
  0.0 0.7 %copy-done.2 = s32[1,1,3]{2,1,0:T(1,128)S(1)} copy-done((s32[1,1,3]{2,1,0:T(1,128)S(1)}, s32[1,1,3]{2,1,0:T(1,128)}, u32[]{:S(2)}) %copy-start.2) | copy-done | bytes 36
  0.7 0.0 copy-done.3
  0.7 0.0 copy-start
  0.7 1.1 %copy-done = f32[1,1,3,256,256]{4,3,2,1,0:T(8,128)S(1)} copy-done((f32[1,1,3,256,256]{4,3,2,1,0:T(8,128)S(1)}, f32[1,1,3,256,256]{4,3,2,1,0:T(8,128)}, u32[]{:S(2)}) %copy-start) | copy-done | bytes 786456
  1.8 0.0 copy-start.1
  1.8 1.1 %copy-done.1 = f32[1,1,3,256,256]{4,3,2,1,0:T(8,128)S(1)} copy-done((f32[1,1,3,256,256]{4,3,2,1,0:T(8,128)S(1)}, f32[1,1,3,256,256]{4,3,2,1,0:T(8,128)}, u32[]{:S(2)}) %copy-start.1) | copy-done | bytes 786456
  2.9 51.4 %shard_map.46 = f32[512,512]{1,0:T(8,128)S(1)} custom-call(f32[3,256,256]{2,1,0:T(8,128)S(1)} %bitcast.4, s32[1,3]{1,0:T(1,128)S(1)} %bitcast.6, f32[3,256,256]{2,1,0:T(8,128)S(1)} %bitcast.5, s32[1,3]{1,0:T(1,128)S(1)} %bitcast.7), custom_call_target="tpu_custom_call" | custom-call | tf_op jit(solution)/shard_map/pallas_call | solution.py:159
  54.4 1.0 %copy.6 = f32[512,512]{1,0:T(8,128)} copy(f32[512,512]{1,0:T(8,128)S(1)} %shard_map.46) | data formatting | bytes 2097152
Async XLA Ops:
  0.0 0.7 %copy-start.2 = (s32[1,1,3]{2,1,0:T(1,128)S(1)}, s32[1,1,3]{2,1,0:T(1,128)}, u32[]{:S(2)}) copy-start(s32[1,1,3]{2,1,0:T(1,128)} %param.5) | copy-start | bytes 40
  0.0 0.7 %copy-start.3 = (s32[1,1,3]{2,1,0:T(1,128)S(1)}, s32[1,1,3]{2,1,0:T(1,128)}, u32[]{:S(2)}) copy-start(s32[1,1,3]{2,1,0:T(1,128)} %param.7) | copy-start | bytes 40
  0.7 1.1 %copy-start = (f32[1,1,3,256,256]{4,3,2,1,0:T(8,128)S(1)}, f32[1,1,3,256,256]{4,3,2,1,0:T(8,128)}, u32[]{:S(2)}) copy-start(f32[1,1,3,256,256]{4,3,2,1,0:T(8,128)} %param.4) | copy-start | bytes 2359300
  1.8 1.1 %copy-start.1 = (f32[1,1,3,256,256]{4,3,2,1,0:T(8,128)S(1)}, f32[1,1,3,256,256]{4,3,2,1,0:T(8,128)}, u32[]{:S(2)}) copy-start(f32[1,1,3,256,256]{4,3,2,1,0:T(8,128)} %param.6) | copy-start | bytes 2359300

commit v2 on v1

v2 whole, which is shorter than its diff:
```python
import jax
import jax.numpy as jnp
from jax import lax
from jax.experimental import pallas as pl
from jax.experimental.pallas import tpu as pltpu
from jax.sharding import PartitionSpec as P

BLK = 256
TB = 2
SLOTS = 3
SIDE = BLK * TB
MESH = pl.DeviceIdType.MESH


def place():
    r, c = lax.axis_index("row"), lax.axis_index("col")
    return r // 4, c % 8, (r // 2) % 2 * 4 + c // 8, r % 2


def device(x, y, z, core):
    return (x * 4 + z // 4 * 2 + core, z % 4 * 8 + y)


def along(rows, cols):
    r, c = lax.axis_index("row"), lax.axis_index("col")
    return ((r + rows) % 32, (c + cols) % 32)


def signal(sem, target):
    pl.semaphore_signal(sem, inc=1, device_id=target, device_id_type=MESH)


def start(copies):
    for copy in copies:
        copy.start()


def halves(block):
    top = block.astype(jnp.bfloat16)
    return top, (block - top.astype(jnp.float32)).astype(jnp.bfloat16)


def densify(slots, where, high, low):
    positions = where[...]
    for p in range(TB * TB):
        r, k = p // TB, p % TB
        chosen = [(positions[:, s : s + 1] == p).astype(jnp.float32) for s in range(SLOTS)]
        block = chosen[0] * slots[0] + chosen[1] * slots[1] + chosen[2] * slots[2]
        spot = (pl.ds(r * BLK, BLK), pl.ds(k * BLK, BLK))
        high[spot], low[spot] = halves(block)


def three_dots(lh, ll, rh, rl):
    def dot(u, v):
        return jnp.dot(u, v, preferred_element_type=jnp.float32)

    return dot(lh, rh) + dot(lh, rl) + dot(ll, rh)


def kernel(
    a, a_pos, b, b_pos, out, a_own, b_own, a_in, b_in, passing, where, tiles, load, send, recv, relay, ready, ready_wrap, ready_last
):
    x, y, z, core = place()
    lo = z % 4
    far = core == 0
    upper = z >= 4
    barrier = pltpu.get_barrier_semaphore()

    local = [
        pltpu.make_async_copy(a, a_own, load.at[0]),
        pltpu.make_async_copy(b, b_own, load.at[1]),
        pltpu.make_async_copy(a_pos, where.at[0], load.at[2]),
        pltpu.make_async_copy(b_pos, where.at[1], load.at[3]),
    ]
    start(local)

    wrap = y == 0
    detour = jnp.where(far, 1, 6)
    aside = y == detour
    onward = jnp.logical_or(wrap, aside)
    arriving = jnp.logical_or(onward, y == 7)
    z_to = jnp.where(lo == 0, z + 3, z - 1)
    z_from = jnp.where(lo == 3, z - 3, z + 1)
    wrap_to = [device(x, 7, z_to, core), device(x, 0, z_to, core), device(x, detour, z_to, core)]
    wrap_from = device(x, 0, z_from, core)
    last = device(x, 7, z, core)
    a_to, a_from = along(0, -1), along(0, 1)
    b_to, b_from = along(-1, 0), along(1, 0)

    def remote(src, dst, ss, rs, target):
        return pltpu.make_async_remote_copy(
            src_ref=src, dst_ref=dst, send_sem=ss, recv_sem=rs, device_id=target, device_id_type=MESH
        )

    def to_slot(src, which, slot, target):
        dst = (a_in, b_in)[which].at[slot]
        return remote(src, dst, send.at[which, slot], recv.at[which, slot], target)

    a_places = remote(a_pos, where.at[2], send.at[0, SLOTS], recv.at[0, SLOTS], a_to)
    b_places = remote(b_pos, where.at[3], send.at[1, SLOTS], recv.at[1, SLOTS], b_to)
    a_sends = [to_slot(a.at[s], 0, s, a_to) for s in range(SLOTS)]
    b_sends = [to_slot(b.at[s], 1, s, b_to) for s in range(SLOTS)]
    step = [remote(a.at[s], passing, send.at[0, s], relay.at[0], wrap_to[s]) for s in (1, 2)]
    slot = jnp.where(wrap, 1, 2)
    forward = remote(passing, a_in.at[slot], relay.at[1], recv.at[0, slot], last)

    def send_wrapped():
        a_places.start()
        start(step)
        a_sends[0].start()

    late = lo == 3

    @pl.when(y < 7)
    def _():
        signal(barrier, a_from)

    @pl.when(jnp.logical_and(arriving, jnp.logical_not(late)))
    def _():
        signal(barrier, wrap_from)

    @pl.when(jnp.logical_and(wrap, lo == 0))
    def _():
        for target in wrap_to:
            signal(barrier, target)

    @pl.when(jnp.logical_or(wrap, jnp.logical_and(y == 1, far)))
    def _():
        signal(barrier, last)

    @pl.when(jnp.logical_or(jnp.logical_not(far), jnp.logical_not(upper)))
    def _():
        signal(barrier, b_to)

    @pl.when(jnp.logical_and(jnp.logical_not(far), jnp.logical_not(upper)))
    def _():
        signal(barrier, b_from)

    def count(condition, number=1):
        return jnp.where(condition, number, 0)

    need = count(y > 0) + count(jnp.logical_and(wrap, lo > 0), 3) + count(far) + count(upper)
    need += count(y == 7, 1 + count(far)) + count(jnp.logical_and(arriving, late))

    @pl.when(need > 0)
    def _():
        pl.semaphore_wait(barrier, need)

    @pl.when(jnp.logical_or(far, upper))
    def _():
        signal(ready, b_from)

    @pl.when(jnp.logical_and(far, upper))
    def _():
        b_places.start()
        start(b_sends)

    @pl.when(jnp.logical_and(arriving, late))
    def _():
        signal(ready_wrap, wrap_from)

    @pl.when(y == 7)
    def _():
        signal(ready_last, device(x, 0, z, core))
        signal(ready_last, device(x, detour, z, core))

    @pl.when(y > 0)
    def _():
        a_places.start()
        start(a_sends)

    @pl.when(jnp.logical_and(wrap, lo > 0))
    def _():
        send_wrapped()

    @pl.when(jnp.logical_not(far))
    def _():
        pl.semaphore_wait(ready, 1)
        b_places.start()
        start(b_sends)

    for copy in local:
        copy.wait()
    ah, al, bh, bl = (tiles.at[i] for i in range(4))
    densify(a_own, where.at[0], ah, al)
    densify(b_own, where.at[1], bh, bl)
    for c in range(TB):
        cols = pl.ds(c * BLK, BLK)
        out[:, cols] = three_dots(ah[...], al[...], bh[:, cols], bl[:, cols])

    @pl.when(jnp.logical_and(wrap, lo == 0))
    def _():
        pl.semaphore_wait(ready_wrap, SLOTS)
        send_wrapped()

    @pl.when(jnp.logical_and(far, jnp.logical_not(upper)))
    def _():
        pl.semaphore_wait(ready, 1)
        b_places.start()
        start(b_sends)

    @pl.when(onward)
    def _():
        pl.semaphore_wait(ready_last, 1)
        step[0].wait_recv()
        forward.start()

    for copy in [a_places] + a_sends:
        copy.wait_recv()
    densify(a_in, where.at[2], ah, al)
    b_places.wait_recv()
    positions = where[3]
    for s in range(SLOTS):
        row = positions[:, s : s + 1] // TB
        picked = [jnp.where(row == 0, t[:, :BLK], jnp.where(row == 1, t[:, BLK:], 0)) for t in (ah[...], al[...])]
        b_sends[s].wait_recv()
        term = three_dots(*picked, *halves(b_in[s]))
        for c in range(TB):
            here = jnp.logical_and(positions[:, s : s + 1] % TB == c, row < TB).astype(jnp.float32)
            out[:, pl.ds(c * BLK, BLK)] += here * term

    for copy in [a_places, b_places] + a_sends + b_sends:
        copy.wait_send()

    @pl.when(onward)
    def _():
        forward.wait_send()


def body(a_blocks, a_positions, b_blocks, b_positions):
    held = pltpu.VMEM((SLOTS, BLK, BLK), jnp.float32)
    inputs = (a_blocks[0, 0], a_positions[0], b_blocks[0, 0], b_positions[0])
    return pl.pallas_call(
        kernel,
        out_shape=jax.ShapeDtypeStruct((SIDE, SIDE), jnp.float32),
        in_specs=[pl.BlockSpec(memory_space=pltpu.HBM)] * 4,
        out_specs=pl.BlockSpec(memory_space=pltpu.VMEM),
        scratch_shapes=[
            held,
            held,
            held,
            held,
            pltpu.VMEM((BLK, BLK), jnp.float32),
            pltpu.VMEM((4, 1, SLOTS), jnp.int32),
            pltpu.VMEM((4, SIDE, SIDE), jnp.bfloat16),
            pltpu.SemaphoreType.DMA((4,)),
            pltpu.SemaphoreType.DMA((2, SLOTS + 1)),
            pltpu.SemaphoreType.DMA((2, SLOTS + 1)),
            pltpu.SemaphoreType.DMA((2,)),
            pltpu.SemaphoreType.REGULAR,
            pltpu.SemaphoreType.REGULAR,
            pltpu.SemaphoreType.REGULAR,
        ],
        compiler_params=pltpu.CompilerParams(
            collective_id=0, has_side_effects=True, vmem_limit_bytes=40 * 1024 * 1024
        ),
    )(*(pltpu.with_memory_space_constraint(v, pltpu.HBM) for v in inputs))


def solution(mesh):
    placed = (
        P("row", "col", None, None, None),
        P("row", "col", None),
        P("row", "col", None, None, None),
        P("row", "col", None),
    )
    return jax.shard_map(body, mesh=mesh, in_specs=placed, out_specs=P("row", "col"), check_vma=False)
```

time: 55.6 us -> 43.9 us (0.79)
  the two profiles are of different devices: /device:TPU:115 before, /device:TPU:496 now
where the time goes in v2:
time: 43.9 us; the launch traced here: 43.7 us
  Pallas kernels  42.7 us (97%)
  local copies, waits for them, and re-layouts  0.97 us (2%)
    pallas_call x1, Pallas kernels, body(): pl.pallas_call(kernel, out_shape=jax.ShapeDtypeStruct((SIDE, SIDE), jnp.f...  42.7 us
    unnamed x1, local copies, waits for them, and re-layouts  0.97 us

profile of v2, /device:TPU:496, one launch (start us, length us, event | category | flops | bytes accessed | tf_op | source)
XLA Modules:
  0.0 43.7 jit_solution(3606503409353270925)
XLA Ops:
  0.0 42.7 %shard_map.46 = f32[512,512]{1,0:T(8,128)S(1)} custom-call(f32[3,256,256]{2,1,0:T(8,128)} %bitcast.4, s32[1,3]{1,0:T(1,128)} %bitcast.6, f32[3,256,256]{2,1,0:T(8,128)} %bitcast.5, s32[1,3]{1,0:T(1,128)} %bitcast.7), custom_call_target="tpu_custom_call" | custom-call | tf_op jit(solution)/shard_map/pallas_call | solution.py:233
  42.7 1.0 %copy.6 = f32[512,512]{1,0:T(8,128)} copy(f32[512,512]{1,0:T(8,128)S(1)} %shard_map.46) | data formatting | bytes 2097152

commit v3 on v2

--- a/solution.py
+++ b/solution.py
@@ -9,6 +9,7 @@
 TB = 2
 SLOTS = 3
 SIDE = BLK * TB
+PARTS = 2
 MESH = pl.DeviceIdType.MESH
 
 
@@ -58,7 +59,7 @@
 
 
 def kernel(
-    a, a_pos, b, b_pos, out, a_own, b_own, a_in, b_in, passing, where, tiles, load, send, recv, relay, ready, ready_wrap, ready_last
+    a, a_pos, b, b_pos, out, a_own, b_own, a_in, b_in, passing, where, tiles, load, send, recv, relay, ready, ready_wrap, ready_last, ready_over
 ):
     x, y, z, core = place()
     lo = z % 4
@@ -75,15 +76,21 @@
     start(local)
 
     wrap = y == 0
-    detour = jnp.where(far, 1, 6)
+    detour = jnp.where(far, 1, 2)
     aside = y == detour
-    onward = jnp.logical_or(wrap, aside)
-    arriving = jnp.logical_or(onward, y == 7)
-    z_to = jnp.where(lo == 0, z + 3, z - 1)
-    z_from = jnp.where(lo == 3, z - 3, z + 1)
-    wrap_to = [device(x, 7, z_to, core), device(x, 0, z_to, core), device(x, detour, z_to, core)]
+    inner = jnp.logical_or(wrap, aside)
+    outer = y == 7
+    lower = jnp.logical_not(upper)
+    near = jnp.logical_not(far)
+    early, late = lo == 0, lo == 3
+    first, second = z == 0, z == 1
+    told = jnp.logical_and(wrap, first)
+    z_to = jnp.where(early, z + 3, z - 1)
+    z_from = jnp.where(late, z - 3, z + 1)
+    wrap_to = [device(x, 7, z, core), device(x, 0, z_to, core), device(x, detour, z_to, core)]
     wrap_from = device(x, 0, z_from, core)
     last = device(x, 7, z, core)
+    last_to, last_from = device(x, 7, z_to, core), device(x, 7, z_from, core)
     a_to, a_from = along(0, -1), along(0, 1)
     b_to, b_from = along(-1, 0), along(1, 0)
 
@@ -100,47 +107,67 @@
     b_places = remote(b_pos, where.at[3], send.at[1, SLOTS], recv.at[1, SLOTS], b_to)
     a_sends = [to_slot(a.at[s], 0, s, a_to) for s in range(SLOTS)]
     b_sends = [to_slot(b.at[s], 1, s, b_to) for s in range(SLOTS)]
-    step = [remote(a.at[s], passing, send.at[0, s], relay.at[0], wrap_to[s]) for s in (1, 2)]
-    slot = jnp.where(wrap, 1, 2)
-    forward = remote(passing, a_in.at[slot], relay.at[1], recv.at[0, slot], last)
-
-    def send_wrapped():
-        a_places.start()
-        start(step)
-        a_sends[0].start()
-
-    late = lo == 3
+
+    rows = [pl.ds(i * BLK // PARTS, BLK // PARTS) for i in range(PARTS)]
+    step_places = remote(a_pos, where.at[4], send.at[0, SLOTS], relay.at[2, 0], wrap_to[0])
+    step = [
+        [remote(a.at[s, part], passing.at[part], send.at[0, s], relay.at[0, i], wrap_to[s]) for i, part in enumerate(rows)]
+        for s in range(SLOTS)
+    ]
+    slot = jnp.where(outer, 0, jnp.where(wrap, 1, 2))
+    target = [jnp.where(outer, u, v) for u, v in zip(last_to, last)]
+    pass_places = remote(where.at[4], where.at[2], relay.at[2, 1], recv.at[0, SLOTS], tuple(target))
+    forward = [
+        remote(passing.at[part], a_in.at[slot, part], relay.at[1, i], recv.at[0, slot], tuple(target))
+        for i, part in enumerate(rows)
+    ]
 
     @pl.when(y < 7)
     def _():
         signal(barrier, a_from)
 
-    @pl.when(jnp.logical_and(arriving, jnp.logical_not(late)))
+    @pl.when(jnp.logical_and(inner, jnp.logical_not(jnp.logical_or(late, told))))
     def _():
         signal(barrier, wrap_from)
 
-    @pl.when(jnp.logical_and(wrap, lo == 0))
-    def _():
-        for target in wrap_to:
-            signal(barrier, target)
-
-    @pl.when(jnp.logical_or(wrap, jnp.logical_and(y == 1, far)))
+    @pl.when(jnp.logical_and(wrap, jnp.logical_or(early, second)))
+    def _():
+        signal(barrier, wrap_to[1])
+
+    @pl.when(jnp.logical_and(wrap, early))
+    def _():
+        signal(barrier, wrap_to[2])
+
+    @pl.when(jnp.logical_and(wrap, jnp.logical_not(early)))
+    def _():
+        signal(barrier, last_to)
+
+    @pl.when(jnp.logical_and(outer, early))
+    def _():
+        signal(barrier, last_to)
+
+    @pl.when(jnp.logical_and(inner, jnp.logical_not(told)))
     def _():
         signal(barrier, last)
 
-    @pl.when(jnp.logical_or(jnp.logical_not(far), jnp.logical_not(upper)))
+    @pl.when(jnp.logical_and(outer, first))
+    def _():
+        signal(barrier, device(x, 0, z, core))
+
+    @pl.when(jnp.logical_or(near, lower))
     def _():
         signal(barrier, b_to)
 
-    @pl.when(jnp.logical_and(jnp.logical_not(far), jnp.logical_not(upper)))
+    @pl.when(jnp.logical_and(near, lower))
     def _():
         signal(barrier, b_from)
 
     def count(condition, number=1):
         return jnp.where(condition, number, 0)
 
-    need = count(y > 0) + count(jnp.logical_and(wrap, lo > 0), 3) + count(far) + count(upper)
-    need += count(y == 7, 1 + count(far)) + count(jnp.logical_and(arriving, late))
+    need = count(y > 0) + count(jnp.logical_and(wrap, jnp.logical_not(early)), 2 - count(second))
+    need += count(far) + count(upper) + count(outer, 3 - count(first)) + count(told, 2)
+    need += count(jnp.logical_and(inner, late))
 
     @pl.when(need > 0)
     def _():
@@ -155,58 +182,131 @@
         b_places.start()
         start(b_sends)
 
-    @pl.when(jnp.logical_and(arriving, late))
+    @pl.when(jnp.logical_or(jnp.logical_and(wrap, late), told))
     def _():
         signal(ready_wrap, wrap_from)
 
-    @pl.when(y == 7)
-    def _():
-        signal(ready_last, device(x, 0, z, core))
+    @pl.when(jnp.logical_and(aside, late))
+    def _():
+        signal(ready_over, wrap_from)
+
+    @pl.when(outer)
+    def _():
+        @pl.when(z > 0)
+        def _():
+            signal(ready_last, device(x, 0, z, core))
+
         signal(ready_last, device(x, detour, z, core))
+
+        @pl.when(late)
+        def _():
+            signal(ready_wrap, last_from)
+
+        @pl.when(jnp.logical_not(late))
+        def _():
+            signal(ready_over, wrap_from)
 
     @pl.when(y > 0)
     def _():
         a_places.start()
         start(a_sends)
 
-    @pl.when(jnp.logical_and(wrap, lo > 0))
-    def _():
-        send_wrapped()
-
-    @pl.when(jnp.logical_not(far))
+    @pl.when(jnp.logical_and(wrap, jnp.logical_not(early)))
+    def _():
+        @pl.when(jnp.logical_not(second))
+        def _():
+            start(step[1])
+
+        start(step[2])
+        pl.semaphore_wait(ready_over, 1)
+        a_places.start()
+        a_sends[0].start()
+
+        @pl.when(second)
+        def _():
+            pl.semaphore_wait(ready_wrap, 1)
+            start(step[1])
+
+    @pl.when(jnp.logical_and(wrap, early))
+    def _():
+        @pl.when(z > 0)
+        def _():
+            pl.semaphore_wait(ready_last, 1)
+
+        step_places.start()
+        start(step[0])
+        pl.semaphore_wait(ready_wrap, 1)
+        start(step[1])
+        pl.semaphore_wait(ready_over, 1)
+        start(step[2])
+
+    @pl.when(near)
     def _():
         pl.semaphore_wait(ready, 1)
         b_places.start()
         start(b_sends)
 
-    for copy in local:
-        copy.wait()
-    ah, al, bh, bl = (tiles.at[i] for i in range(4))
-    densify(a_own, where.at[0], ah, al)
-    densify(b_own, where.at[1], bh, bl)
-    for c in range(TB):
-        cols = pl.ds(c * BLK, BLK)
-        out[:, cols] = three_dots(ah[...], al[...], bh[:, cols], bl[:, cols])
-
-    @pl.when(jnp.logical_and(wrap, lo == 0))
-    def _():
-        pl.semaphore_wait(ready_wrap, SLOTS)
-        send_wrapped()
-
-    @pl.when(jnp.logical_and(far, jnp.logical_not(upper)))
+    def pass_on():
+        for one, other in zip(step[0], forward):
+            one.wait_recv()
+            other.start()
+
+    @pl.when(jnp.logical_and(outer, early))
+    def _():
+        pl.semaphore_wait(ready_wrap, 1)
+        step_places.wait_recv()
+        pass_places.start()
+        pass_on()
+
+    held_up = jnp.logical_and(jnp.logical_and(far, lower), jnp.logical_and(z >= 2, jnp.logical_and(y > 0, y < 7)))
+
+    @pl.when(jnp.logical_and(far, lower))
     def _():
         pl.semaphore_wait(ready, 1)
+
+        @pl.when(held_up)
+        def _():
+            a_sends[0].wait_recv()
+            a_sends[1].wait_recv()
+
         b_places.start()
         start(b_sends)
 
-    @pl.when(onward)
+    @pl.when(jnp.logical_or(aside, jnp.logical_and(wrap, jnp.logical_not(early))))
     def _():
         pl.semaphore_wait(ready_last, 1)
-        step[0].wait_recv()
-        forward.start()
-
-    for copy in [a_places] + a_sends:
-        copy.wait_recv()
+
+    ah, al, bh, bl = (tiles.at[i] for i in range(4))
+
+    def turn(i, carry):
+        passing_now = (i == 0) != late
+
+        @pl.when(jnp.logical_and(inner, passing_now))
+        def _():
+            pass_on()
+
+        @pl.when(jnp.logical_not(passing_now))
+        def _():
+            for copy in local:
+                copy.wait()
+            densify(a_own, where.at[0], ah, al)
+            densify(b_own, where.at[1], bh, bl)
+            for c in range(TB):
+                cols = pl.ds(c * BLK, BLK)
+                out[:, cols] = three_dots(ah[...], al[...], bh[:, cols], bl[:, cols])
+
+        return carry
+
+    lax.fori_loop(0, 2, turn, 0)
+
+    a_places.wait_recv()
+
+    @pl.when(jnp.logical_not(held_up))
+    def _():
+        a_sends[0].wait_recv()
+        a_sends[1].wait_recv()
+
+    a_sends[2].wait_recv()
     densify(a_in, where.at[2], ah, al)
     b_places.wait_recv()
     positions = where[3]
@@ -222,9 +322,14 @@
     for copy in [a_places, b_places] + a_sends + b_sends:
         copy.wait_send()
 
-    @pl.when(onward)
-    def _():
-        forward.wait_send()
+    @pl.when(jnp.logical_or(inner, jnp.logical_and(outer, early)))
+    def _():
+        for copy in forward:
+            copy.wait_send()
+
+    @pl.when(jnp.logical_and(outer, early))
+    def _():
+        pass_places.wait_send()
 
 
 def body(a_blocks, a_positions, b_blocks, b_positions):
@@ -241,12 +346,13 @@
             held,
             held,
             pltpu.VMEM((BLK, BLK), jnp.float32),
-            pltpu.VMEM((4, 1, SLOTS), jnp.int32),
+            pltpu.VMEM((5, 1, SLOTS), jnp.int32),
             pltpu.VMEM((4, SIDE, SIDE), jnp.bfloat16),
             pltpu.SemaphoreType.DMA((4,)),
             pltpu.SemaphoreType.DMA((2, SLOTS + 1)),
             pltpu.SemaphoreType.DMA((2, SLOTS + 1)),
-            pltpu.SemaphoreType.DMA((2,)),
+            pltpu.SemaphoreType.DMA((3, PARTS)),
+            pltpu.SemaphoreType.REGULAR,
             pltpu.SemaphoreType.REGULAR,
             pltpu.SemaphoreType.REGULAR,
             pltpu.SemaphoreType.REGULAR,

time: 43.9 us -> 40.2 us (0.916)
  the two profiles are of different devices: /device:TPU:496 before, /device:TPU:271 now
where the time goes in v3:
time: 40.2 us; the launch traced here: 40.1 us
  Pallas kernels  39.1 us (97%)
  local copies, waits for them, and re-layouts  0.97 us (2%)
    pallas_call x1, Pallas kernels, body(): pl.pallas_call(kernel, out_shape=jax.ShapeDtypeStruct((SIDE, SIDE), jnp.f...  39.1 us
    unnamed x1, local copies, waits for them, and re-layouts  0.97 us

profile of v3, /device:TPU:271, one launch (start us, length us, event | category | flops | bytes accessed | tf_op | source)
XLA Modules:
  0.0 40.1 jit_solution(9341681850594528939)
XLA Ops:
  0.0 39.1 %shard_map.46 = f32[512,512]{1,0:T(8,128)S(1)} custom-call(f32[3,256,256]{2,1,0:T(8,128)} %bitcast.4, s32[1,3]{1,0:T(1,128)} %bitcast.6, f32[3,256,256]{2,1,0:T(8,128)} %bitcast.5, s32[1,3]{1,0:T(1,128)} %bitcast.7), custom_call_target="tpu_custom_call" | custom-call | tf_op jit(solution)/shard_map/pallas_call | solution.py:338
  39.1 1.0 %copy.6 = f32[512,512]{1,0:T(8,128)} copy(f32[512,512]{1,0:T(8,128)S(1)} %shard_map.46) | data formatting | bytes 2097152

commit v4 on v3

--- a/solution.py
+++ b/solution.py
@@ -59,7 +59,7 @@
 
 
 def kernel(
-    a, a_pos, b, b_pos, out, a_own, b_own, a_in, b_in, passing, where, tiles, load, send, recv, relay, ready, ready_wrap, ready_last, ready_over
+    a, a_pos, b, b_pos, out, a_own, b_own, a_in, b_in, passing, where, tiles, load, send, recv, relay, ready, ready_wrap, ready_last, ready_over, ready_next
 ):
     x, y, z, core = place()
     lo = z % 4
@@ -78,13 +78,22 @@
     wrap = y == 0
     detour = jnp.where(far, 1, 2)
     aside = y == detour
-    inner = jnp.logical_or(wrap, aside)
     outer = y == 7
     lower = jnp.logical_not(upper)
     near = jnp.logical_not(far)
     early, late = lo == 0, lo == 3
-    first, second = z == 0, z == 1
+    first = z == 0
     told = jnp.logical_and(wrap, first)
+    corner = jnp.logical_and(jnp.logical_and(wrap, far), x == 0)
+    zero, spared = jnp.logical_and(corner, first), jnp.logical_and(corner, z == 1)
+    to_zero = jnp.logical_and(jnp.logical_and(wrap, near), jnp.logical_and(z == 4, x == 7))
+    inner = jnp.logical_and(jnp.logical_or(wrap, aside), jnp.logical_not(zero))
+    after_zero = jnp.logical_and(jnp.logical_and(inner, far), jnp.logical_and(z == 3, x == 0))
+    indirect = jnp.logical_or(early, upper)
+    direct = jnp.logical_not(indirect)
+    from_zero = jnp.logical_and(jnp.logical_and(first, far), x == 0)
+    handing = jnp.logical_and(jnp.logical_and(outer, indirect), jnp.logical_not(from_zero))
+    end_of_zero = jnp.logical_and(jnp.logical_and(outer, far), jnp.logical_and(z == 3, x == 0))
     z_to = jnp.where(early, z + 3, z - 1)
     z_from = jnp.where(late, z - 3, z + 1)
     wrap_to = [device(x, 7, z, core), device(x, 0, z_to, core), device(x, detour, z_to, core)]
@@ -122,30 +131,39 @@
         for i, part in enumerate(rows)
     ]
 
-    @pl.when(y < 7)
+    @pl.when(y < 4)
     def _():
         signal(barrier, a_from)
 
-    @pl.when(jnp.logical_and(inner, jnp.logical_not(jnp.logical_or(late, told))))
+    @pl.when(y > 4)
+    def _():
+        signal(barrier, a_to)
+
+    @pl.when(jnp.logical_and(inner, jnp.logical_or(jnp.logical_not(late), after_zero)))
     def _():
         signal(barrier, wrap_from)
 
-    @pl.when(jnp.logical_and(wrap, jnp.logical_or(early, second)))
+    @pl.when(jnp.logical_and(wrap, jnp.logical_and(early, jnp.logical_not(zero))))
     def _():
         signal(barrier, wrap_to[1])
-
-    @pl.when(jnp.logical_and(wrap, early))
-    def _():
         signal(barrier, wrap_to[2])
 
-    @pl.when(jnp.logical_and(wrap, jnp.logical_not(early)))
+    @pl.when(jnp.logical_and(wrap, direct))
     def _():
         signal(barrier, last_to)
 
-    @pl.when(jnp.logical_and(outer, early))
+    @pl.when(jnp.logical_and(outer, jnp.logical_and(upper, jnp.logical_not(late))))
+    def _():
+        signal(barrier, last_from)
+
+    @pl.when(jnp.logical_and(handing, early))
     def _():
         signal(barrier, last_to)
 
+    @pl.when(end_of_zero)
+    def _():
+        signal(barrier, wrap_from)
+
     @pl.when(jnp.logical_and(inner, jnp.logical_not(told)))
     def _():
         signal(barrier, last)
@@ -154,39 +172,41 @@
     def _():
         signal(barrier, device(x, 0, z, core))
 
-    @pl.when(jnp.logical_or(near, lower))
+    @pl.when(jnp.logical_and(jnp.logical_or(near, lower), jnp.logical_not(zero)))
     def _():
         signal(barrier, b_to)
 
-    @pl.when(jnp.logical_and(near, lower))
+    @pl.when(jnp.logical_and(near, jnp.logical_or(lower, to_zero)))
     def _():
         signal(barrier, b_from)
 
     def count(condition, number=1):
         return jnp.where(condition, number, 0)
 
-    need = count(y > 0) + count(jnp.logical_and(wrap, jnp.logical_not(early)), 2 - count(second))
-    need += count(far) + count(upper) + count(outer, 3 - count(first)) + count(told, 2)
+    replying = jnp.logical_and(y >= 4, y < 7)
+    need = count(jnp.logical_and(y > 0, y < 5)) + count(replying) + count(jnp.logical_and(wrap, jnp.logical_not(early)), 2 - count(spared))
+    need += count(far) + count(upper) - count(to_zero) + count(zero, 4) + count(told) - count(after_zero)
+    need += count(outer, 2 - count(first) + count(z < 3) + count(late) + count(z > 4)) - count(end_of_zero)
     need += count(jnp.logical_and(inner, late))
 
     @pl.when(need > 0)
     def _():
         pl.semaphore_wait(barrier, need)
 
-    @pl.when(jnp.logical_or(far, upper))
+    @pl.when(jnp.logical_and(jnp.logical_or(far, upper), jnp.logical_not(to_zero)))
     def _():
         signal(ready, b_from)
 
-    @pl.when(jnp.logical_and(far, upper))
+    @pl.when(jnp.logical_and(far, jnp.logical_or(upper, zero)))
     def _():
         b_places.start()
         start(b_sends)
 
-    @pl.when(jnp.logical_or(jnp.logical_and(wrap, late), told))
+    @pl.when(jnp.logical_and(wrap, jnp.logical_and(late, jnp.logical_not(after_zero))))
     def _():
         signal(ready_wrap, wrap_from)
 
-    @pl.when(jnp.logical_and(aside, late))
+    @pl.when(jnp.logical_and(aside, jnp.logical_and(late, jnp.logical_not(after_zero))))
     def _():
         signal(ready_over, wrap_from)
 
@@ -198,69 +218,106 @@
 
         signal(ready_last, device(x, detour, z, core))
 
-        @pl.when(late)
+        @pl.when(jnp.logical_and(late, jnp.logical_not(end_of_zero)))
         def _():
             signal(ready_wrap, last_from)
 
-        @pl.when(jnp.logical_not(late))
+        @pl.when(z < 3)
         def _():
             signal(ready_over, wrap_from)
+
+    @pl.when(replying)
+    def _():
+        signal(ready_next, a_from)
+
+    @pl.when(y > 4)
+    def _():
+        pl.semaphore_wait(ready_next, 1)
 
     @pl.when(y > 0)
     def _():
         a_places.start()
         start(a_sends)
 
-    @pl.when(jnp.logical_and(wrap, jnp.logical_not(early)))
-    def _():
-        @pl.when(jnp.logical_not(second))
-        def _():
-            start(step[1])
-
-        start(step[2])
-        pl.semaphore_wait(ready_over, 1)
-        a_places.start()
-        a_sends[0].start()
-
-        @pl.when(second)
-        def _():
-            pl.semaphore_wait(ready_wrap, 1)
-            start(step[1])
-
-    @pl.when(jnp.logical_and(wrap, early))
-    def _():
-        @pl.when(z > 0)
-        def _():
-            pl.semaphore_wait(ready_last, 1)
-
-        step_places.start()
-        start(step[0])
-        pl.semaphore_wait(ready_wrap, 1)
-        start(step[1])
-        pl.semaphore_wait(ready_over, 1)
-        start(step[2])
-
-    @pl.when(near)
-    def _():
+    def send_near():
         pl.semaphore_wait(ready, 1)
         b_places.start()
         start(b_sends)
+
+    @pl.when(jnp.logical_and(wrap, jnp.logical_not(early)))
+    def _():
+        @pl.when(jnp.logical_not(spared))
+        def _():
+            start(step[1])
+
+        start(step[2])
+
+        @pl.when(upper)
+        def _():
+            pl.semaphore_wait(ready_last, 1)
+            step_places.start()
+            start(step[0])
+
+        @pl.when(lower)
+        def _():
+            pl.semaphore_wait(ready_over, 1)
+            a_places.start()
+            a_sends[0].start()
+
+        @pl.when(spared)
+        def _():
+            a_sends[1].start()
+
+    @pl.when(jnp.logical_and(wrap, early))
+    def _():
+        @pl.when(z > 0)
+        def _():
+            pl.semaphore_wait(ready_last, 1)
+
+        @pl.when(zero)
+        def _():
+            a_places.start()
+            a_sends[0].start()
+
+        @pl.when(jnp.logical_not(zero))
+        def _():
+            step_places.start()
+            start(step[0])
+            pl.semaphore_wait(ready_wrap, 1)
+
+        start(step[1])
+
+        @pl.when(jnp.logical_not(zero))
+        def _():
+            pl.semaphore_wait(ready_over, 1)
+
+        start(step[2])
+
+    @pl.when(near)
+    def _():
+        send_near()
 
     def pass_on():
         for one, other in zip(step[0], forward):
             one.wait_recv()
             other.start()
 
-    @pl.when(jnp.logical_and(outer, early))
-    def _():
-        pl.semaphore_wait(ready_wrap, 1)
+    def hand_on():
+        @pl.when(early)
+        def _():
+            pl.semaphore_wait(ready_wrap, 1)
+
         step_places.wait_recv()
         pass_places.start()
         pass_on()
 
-    held_up = jnp.logical_and(jnp.logical_and(far, lower), jnp.logical_and(z >= 2, jnp.logical_and(y > 0, y < 7)))
-
-    @pl.when(jnp.logical_and(far, lower))
+    @pl.when(handing)
+    def _():
+        hand_on()
+
+    held_up = jnp.logical_and(jnp.logical_and(far, lower), jnp.logical_and(z >= 2, y < 7))
+
+    @pl.when(jnp.logical_and(jnp.logical_and(far, lower), jnp.logical_not(zero)))
     def _():
         pl.semaphore_wait(ready, 1)
 
@@ -272,14 +329,14 @@
         b_places.start()
         start(b_sends)
 
-    @pl.when(jnp.logical_or(aside, jnp.logical_and(wrap, jnp.logical_not(early))))
+    @pl.when(jnp.logical_or(aside, jnp.logical_and(wrap, direct)))
     def _():
         pl.semaphore_wait(ready_last, 1)
 
     ah, al, bh, bl = (tiles.at[i] for i in range(4))
 
     def turn(i, carry):
-        passing_now = (i == 0) != late
+        passing_now = (i == 0) != jnp.logical_or(late, upper)
 
         @pl.when(jnp.logical_and(inner, passing_now))
         def _():
@@ -322,12 +379,12 @@
     for copy in [a_places, b_places] + a_sends + b_sends:
         copy.wait_send()
 
-    @pl.when(jnp.logical_or(inner, jnp.logical_and(outer, early)))
+    @pl.when(jnp.logical_or(inner, handing))
     def _():
         for copy in forward:
             copy.wait_send()
 
-    @pl.when(jnp.logical_and(outer, early))
+    @pl.when(handing)
     def _():
         pass_places.wait_send()
 
@@ -356,6 +413,7 @@
             pltpu.SemaphoreType.REGULAR,
             pltpu.SemaphoreType.REGULAR,
             pltpu.SemaphoreType.REGULAR,
+            pltpu.SemaphoreType.REGULAR,
         ],
         compiler_params=pltpu.CompilerParams(
             collective_id=0, has_side_effects=True, vmem_limit_bytes=40 * 1024 * 1024

time: 40.2 us -> 38.4 us (0.955)
  the two profiles are of different devices: /device:TPU:271 before, /device:TPU:496 now
where the time goes in v4:
time: 38.4 us; the launch traced here: 38.2 us
  Pallas kernels  37.3 us (97%)
  local copies, waits for them, and re-layouts  0.97 us (3%)
    pallas_call x1, Pallas kernels, body(): pl.pallas_call(kernel, out_shape=jax.ShapeDtypeStruct((SIDE, SIDE), jnp.f...  37.3 us
    unnamed x1, local copies, waits for them, and re-layouts  0.97 us

profile of v4, /device:TPU:496, one launch (start us, length us, event | category | flops | bytes accessed | tf_op | source)
XLA Modules:
  0.0 38.2 jit_solution(4889429926673992533)
XLA Ops:
  0.0 37.3 %shard_map.46 = f32[512,512]{1,0:T(8,128)S(1)} custom-call(f32[3,256,256]{2,1,0:T(8,128)} %bitcast.4, s32[1,3]{1,0:T(1,128)} %bitcast.6, f32[3,256,256]{2,1,0:T(8,128)} %bitcast.5, s32[1,3]{1,0:T(1,128)} %bitcast.7), custom_call_target="tpu_custom_call" | custom-call | tf_op jit(solution)/shard_map/pallas_call | solution.py:395
  37.3 1.0 %copy.6 = f32[512,512]{1,0:T(8,128)} copy(f32[512,512]{1,0:T(8,128)S(1)} %shard_map.46) | data formatting | bytes 2097152

commit v5 on v4

--- a/solution.py
+++ b/solution.py
@@ -268,6 +268,17 @@
         def _():
             a_sends[1].start()
 
+    @pl.when(jnp.logical_and(near, upper))
+    def _():
+        send_near()
+
+    waiting = jnp.logical_and(wrap, z == 4)
+
+    @pl.when(waiting)
+    def _():
+        for copy in a_sends[:2]:
+            copy.wait_recv()
+
     @pl.when(jnp.logical_and(wrap, early))
     def _():
         @pl.when(z > 0)
@@ -293,7 +304,7 @@
 
         start(step[2])
 
-    @pl.when(near)
+    @pl.when(jnp.logical_and(near, lower))
     def _():
         send_near()
 
@@ -311,11 +322,12 @@
         pass_places.start()
         pass_on()
 
-    @pl.when(handing)
+    @pl.when(jnp.logical_and(handing, z != 4))
     def _():
         hand_on()
 
     held_up = jnp.logical_and(jnp.logical_and(far, lower), jnp.logical_and(z >= 2, y < 7))
+    held_last = jnp.logical_and(jnp.logical_and(far, lower), jnp.logical_and(z >= 2, outer))
 
     @pl.when(jnp.logical_and(jnp.logical_and(far, lower), jnp.logical_not(zero)))
     def _():
@@ -326,6 +338,11 @@
             a_sends[0].wait_recv()
             a_sends[1].wait_recv()
 
+        @pl.when(held_last)
+        def _():
+            for copy in a_sends:
+                copy.wait_send()
+
         b_places.start()
         start(b_sends)
 
@@ -341,6 +358,10 @@
         @pl.when(jnp.logical_and(inner, passing_now))
         def _():
             pass_on()
+
+        @pl.when(jnp.logical_and(jnp.logical_and(handing, z == 4), passing_now))
+        def _():
+            hand_on()
 
         @pl.when(jnp.logical_not(passing_now))
         def _():
@@ -356,27 +377,53 @@
 
     lax.fori_loop(0, 2, turn, 0)
 
-    a_places.wait_recv()
-
-    @pl.when(jnp.logical_not(held_up))
-    def _():
-        a_sends[0].wait_recv()
-        a_sends[1].wait_recv()
-
-    a_sends[2].wait_recv()
-    densify(a_in, where.at[2], ah, al)
-    b_places.wait_recv()
-    positions = where[3]
-    for s in range(SLOTS):
-        row = positions[:, s : s + 1] // TB
-        picked = [jnp.where(row == 0, t[:, :BLK], jnp.where(row == 1, t[:, BLK:], 0)) for t in (ah[...], al[...])]
-        b_sends[s].wait_recv()
-        term = three_dots(*picked, *halves(b_in[s]))
-        for c in range(TB):
-            here = jnp.logical_and(positions[:, s : s + 1] % TB == c, row < TB).astype(jnp.float32)
-            out[:, pl.ds(c * BLK, BLK)] += here * term
-
-    for copy in [a_places, b_places] + a_sends + b_sends:
+    a_last = jnp.logical_and(outer, jnp.logical_or(upper, jnp.logical_and(late, far)))
+
+    @pl.when(a_last)
+    def _():
+        b_places.wait_recv()
+        for copy in b_sends:
+            copy.wait_recv()
+        densify(b_in, where.at[3], bh, bl)
+        a_places.wait_recv()
+        positions = where[2]
+        for s in range(SLOTS):
+            row = positions[:, s : s + 1] // TB
+            col = positions[:, s : s + 1] % TB
+            picked = [jnp.where(col == 0, t[:BLK], t[BLK:]) for t in (bh[...], bl[...])]
+            a_sends[s].wait_recv()
+            term = three_dots(*halves(a_in[s]), *picked)
+            for r in range(TB):
+                out[pl.ds(r * BLK, BLK), :] += (row == r).astype(jnp.float32) * term
+
+    @pl.when(jnp.logical_not(a_last))
+    def _():
+        a_places.wait_recv()
+
+        @pl.when(jnp.logical_not(jnp.logical_or(held_up, waiting)))
+        def _():
+            a_sends[0].wait_recv()
+            a_sends[1].wait_recv()
+
+        a_sends[2].wait_recv()
+        densify(a_in, where.at[2], ah, al)
+        b_places.wait_recv()
+        positions = where[3]
+        for s in range(SLOTS):
+            row = positions[:, s : s + 1] // TB
+            picked = [jnp.where(row == 0, t[:, :BLK], jnp.where(row == 1, t[:, BLK:], 0)) for t in (ah[...], al[...])]
+            b_sends[s].wait_recv()
+            term = three_dots(*picked, *halves(b_in[s]))
+            for c in range(TB):
+                here = jnp.logical_and(positions[:, s : s + 1] % TB == c, row < TB).astype(jnp.float32)
+                out[:, pl.ds(c * BLK, BLK)] += here * term
+
+    @pl.when(jnp.logical_not(held_last))
+    def _():
+        for copy in a_sends:
+            copy.wait_send()
+
+    for copy in [a_places, b_places] + b_sends:
         copy.wait_send()
 
     @pl.when(jnp.logical_or(inner, handing))

time: 38.4 us -> 35.9 us (0.935)
  the two profiles are of different devices: /device:TPU:496 before, /device:TPU:287 now
where the time goes in v5:
time: 35.9 us; the launch traced here: 35.8 us
  Pallas kernels  34.8 us (97%)
  local copies, waits for them, and re-layouts  0.97 us (3%)
    pallas_call x1, Pallas kernels, body(): pl.pallas_call(kernel, out_shape=jax.ShapeDtypeStruct((SIDE, SIDE), jnp.f...  34.8 us
    unnamed x1, local copies, waits for them, and re-layouts  0.97 us

profile of v5, /device:TPU:287, one launch (start us, length us, event | category | flops | bytes accessed | tf_op | source)
XLA Modules:
  0.0 35.8 jit_solution(956038252934205638)
XLA Ops:
  0.0 34.8 %shard_map.46 = f32[512,512]{1,0:T(8,128)S(1)} custom-call(f32[3,256,256]{2,1,0:T(8,128)} %bitcast.4, s32[1,3]{1,0:T(1,128)} %bitcast.6, f32[3,256,256]{2,1,0:T(8,128)} %bitcast.5, s32[1,3]{1,0:T(1,128)} %bitcast.7), custom_call_target="tpu_custom_call" | custom-call | tf_op jit(solution)/shard_map/pallas_call | solution.py:442
  34.8 1.0 %copy.6 = f32[512,512]{1,0:T(8,128)} copy(f32[512,512]{1,0:T(8,128)S(1)} %shard_map.46) | data formatting | bytes 2097152

commit v6 on v5

--- a/solution.py
+++ b/solution.py
@@ -326,8 +326,8 @@
     def _():
         hand_on()
 
-    held_up = jnp.logical_and(jnp.logical_and(far, lower), jnp.logical_and(z >= 2, y < 7))
-    held_last = jnp.logical_and(jnp.logical_and(far, lower), jnp.logical_and(z >= 2, outer))
+    held_up = jnp.logical_and(jnp.logical_and(far, lower), jnp.logical_and(z >= 2, wrap))
+    held_last = jnp.logical_and(jnp.logical_and(far, lower), jnp.logical_and(z >= 2, y > 0))
 
     @pl.when(jnp.logical_and(jnp.logical_and(far, lower), jnp.logical_not(zero)))
     def _():
@@ -337,6 +337,10 @@
         def _():
             a_sends[0].wait_recv()
             a_sends[1].wait_recv()
+
+            @pl.when(late)
+            def _():
+                a_sends[2].wait_recv()
 
         @pl.when(held_last)
         def _():
@@ -405,7 +409,10 @@
             a_sends[0].wait_recv()
             a_sends[1].wait_recv()
 
-        a_sends[2].wait_recv()
+        @pl.when(jnp.logical_not(jnp.logical_and(held_up, late)))
+        def _():
+            a_sends[2].wait_recv()
+
         densify(a_in, where.at[2], ah, al)
         b_places.wait_recv()
         positions = where[3]

time: 35.9 us -> 35.6 us (level)
  the two profiles are of different devices: /device:TPU:287 before, /device:TPU:271 now
where the time goes in v6:
time: 35.6 us; the launch traced here: 35.5 us
  Pallas kernels  34.5 us (97%)
  local copies, waits for them, and re-layouts  0.97 us (3%)
    pallas_call x1, Pallas kernels, body(): pl.pallas_call(kernel, out_shape=jax.ShapeDtypeStruct((SIDE, SIDE), jnp.f...  34.5 us
    unnamed x1, local copies, waits for them, and re-layouts  0.97 us

profile of v6, /device:TPU:271, one launch (start us, length us, event | category | flops | bytes accessed | tf_op | source)
XLA Modules:
  0.0 35.5 jit_solution(1579394543787750996)
XLA Ops:
  0.0 34.5 %shard_map.46 = f32[512,512]{1,0:T(8,128)S(1)} custom-call(f32[3,256,256]{2,1,0:T(8,128)} %bitcast.4, s32[1,3]{1,0:T(1,128)} %bitcast.6, f32[3,256,256]{2,1,0:T(8,128)} %bitcast.5, s32[1,3]{1,0:T(1,128)} %bitcast.7), custom_call_target="tpu_custom_call" | custom-call | tf_op jit(solution)/shard_map/pallas_call | solution.py:449
  34.5 1.0 %copy.6 = f32[512,512]{1,0:T(8,128)} copy(f32[512,512]{1,0:T(8,128)S(1)} %shard_map.46) | data formatting | bytes 2097152

commit v7 on v6

--- a/solution.py
+++ b/solution.py
@@ -52,10 +52,9 @@
 
 
 def three_dots(lh, ll, rh, rl):
-    def dot(u, v):
-        return jnp.dot(u, v, preferred_element_type=jnp.float32)
-
-    return dot(lh, rh) + dot(lh, rl) + dot(ll, rh)
+    left = jnp.concatenate([lh, lh, ll], axis=1)
+    right = jnp.concatenate([rh, rl, rh], axis=0)
+    return jnp.dot(left, right, preferred_element_type=jnp.float32)
 
 
 def kernel(

time: 35.6 us -> 35.6 us (level)
  no operation moved by 1% of the time
where the time goes in v7:
time: 35.6 us; the launch traced here: 35.5 us
  Pallas kernels  34.5 us (97%)
  local copies, waits for them, and re-layouts  0.97 us (3%)
    pallas_call x1, Pallas kernels, body(): pl.pallas_call(kernel, out_shape=jax.ShapeDtypeStruct((SIDE, SIDE), jnp.f...  34.5 us
    unnamed x1, local copies, waits for them, and re-layouts  0.97 us

profile of v7, /device:TPU:271, one launch (start us, length us, event | category | flops | bytes accessed | tf_op | source)
XLA Modules:
  0.0 35.5 jit_solution(5608323976039999579)
XLA Ops:
  0.0 34.5 %shard_map.46 = f32[512,512]{1,0:T(8,128)S(1)} custom-call(f32[3,256,256]{2,1,0:T(8,128)} %bitcast.4, s32[1,3]{1,0:T(1,128)} %bitcast.6, f32[3,256,256]{2,1,0:T(8,128)} %bitcast.5, s32[1,3]{1,0:T(1,128)} %bitcast.7), custom_call_target="tpu_custom_call" | custom-call | tf_op jit(solution)/shard_map/pallas_call | solution.py:448
  34.5 1.0 %copy.6 = f32[512,512]{1,0:T(8,128)} copy(f32[512,512]{1,0:T(8,128)S(1)} %shard_map.46) | data formatting | bytes 2097152
